TPU v7x, 512 devices: a whole 4x8x8 slice. The times are simulated.
512 devices in a mesh: rows: 32 (over x, y), cols: 16 (over z, core).
Axes of the slice: x: 4, y: 8, z: 8, core: 2. Of those that a mesh axis runs over, the one named last changes fastest.
Arguments:
- tiles: bfloat16 [32, 16, 16, 128, 8, 128], P('rows', 'cols'), may hold values from -64 to 64, as said below
- tile_coords: int32 [32, 16, 16, 2], P('rows', 'cols'), may hold values from 0 to 63, as said below
- tile_counts: int32 [32, 16, 1], P('rows', 'cols'), may hold values from 8 to 16, as said below
- factor_two: bfloat16 [131072, 256], P(('cols', 'rows')), may hold values from -6 to 6
- factor_three: bfloat16 [8, 256], replicated, may hold values from -6 to 6
- sketch_two: bfloat16 [256, 256], replicated, may hold values from -0.375 to 0.375
- sketch_three: bfloat16 [256, 256], replicated, may hold values from -0.375 to 0.375
Outputs:
- new_factor: float32 [65536, 256], P(('rows', 'cols'))
Inputs may be any that keep to these rules, and one draw needn't show every extreme that they name: `tile_coords`: column 0 is a mode-1 block within the row group, below 16; column 1 a mode-2 block within the column group, below 64. Slot 0 of device (r, c) is live and has mode-1 block c and mode-2 block r * 2 + 1, so every mode-1 block has a tile. Dead slots hold valid coordinates too. `tile_counts`: every device with column index 0 is full. `tiles`: dead slots hold arbitrary values.
All inputs are finite; a program needn't handle non-finite values.
Results may differ from a plain program's by a relative error of at most 0.0041.
Values may be sent and summed in bfloat16 or wider, within the bound.
A program may use at most 64 MiB of HBM per device.

v0:
```python
import jax
import jax.numpy as jnp
from jax import lax
from jax.sharding import PartitionSpec as P


def per_device(tiles, tile_coords, tile_counts, factor_two, factor_three, sketch_two, sketch_three):
    slot_tiles = tiles[0, 0]
    coords_here = tile_coords[0, 0]
    live_count = tile_counts[0, 0, 0]
    slots = slot_tiles.shape[0]
    tile_size = slot_tiles.shape[1]
    rank_width = sketch_two.shape[1]
    col_count = lax.axis_size("cols")
    grouped = jnp.dot(
        lax.all_gather(factor_two, "rows", axis=0, tiled=True),
        sketch_two,
        preferred_element_type=jnp.float32,
    ).astype(jnp.bfloat16)
    grouped = grouped.reshape(-1, tile_size, rank_width)
    sketched_three = jnp.dot(factor_three, sketch_three, preferred_element_type=jnp.float32).astype(
        jnp.bfloat16
    )
    depth_factor = lax.optimization_barrier(sketched_three).astype(jnp.float32)
    selected = grouped[coords_here[:, 1]]
    product = jnp.einsum("cikj,cja->cika", slot_tiles, selected, preferred_element_type=jnp.float32)
    partial_value = jnp.sum(product * depth_factor[None, None, :, :], axis=2)
    alive = (jnp.arange(slots, dtype=jnp.int32) < live_count).astype(jnp.float32)
    placing = (
        coords_here[:, 0][:, None] == jnp.arange(col_count, dtype=jnp.int32)[None, :]
    ).astype(jnp.float32) * alive[:, None]
    partials = jnp.einsum("cb,cia->bia", placing, partial_value, precision=lax.Precision.HIGHEST)
    received = lax.all_to_all(partials, "cols", split_axis=0, concat_axis=0, tiled=True)
    row_sums = jnp.sum(received, axis=0)
    gram_local = jnp.dot(row_sums.T, row_sums, precision=lax.Precision.HIGHEST)
    gram_matrix = lax.psum(gram_local, ("rows", "cols"))
    chol_factor = jnp.linalg.cholesky(gram_matrix)
    total_rows = tile_size * lax.axis_size("rows") * col_count
    solved = lax.linalg.triangular_solve(chol_factor, row_sums.T, left_side=True, lower=True)
    return solved.T * jnp.sqrt(jnp.float32(total_rows))


def solution(mesh):
    return jax.shard_map(
        per_device,
        mesh=mesh,
        in_specs=(
            P("rows", "cols", None, None, None, None),
            P("rows", "cols", None, None),
            P("rows", "cols", None),
            P(("cols", "rows"), None),
            P(),
            P(),
            P(),
        ),
        out_specs=P(("rows", "cols"), None),
        check_vma=False,
    )
```

profile of v0, /device:TPU:1, one launch (start us, length us, event | category | flops | bytes accessed | tf_op | source)
XLA Modules:
  0.0 514.2 jit_solution(10481004170048284713)
XLA Ops:
  6.5 0.7 all-gather.2.cloned.1.call-update
  8.0 1.1 convolution_convert_fusion.1
  9.0 0.8 slice_bitcast_fusion.4
  9.8 90.7 %all-gather.2.cloned.1.call-done = bf16[8192,256]{1,0:T(8,128)(2,1)} async-done(((bf16[256,256]{1,0:T(8,128)(2,1)}), bf16[8192,256]{1,0:T(8,128)(2,1)}) %all-gather.2.cloned.1.call-update) | async-done | bytes 4194320 | tf_op jit(solution)/shard_map/all_gather | solution.py:16
  100.5 5.4 %convolution_convert_fusion = bf16[8192,256]{1,0:T(8,128)(2,1)} fusion(bf16[8192,256]{1,0:T(8,128)(2,1)} %all-gather.2.cloned.1.call-done, bf16[256,256]{1,0:T(8,128)(2,1)S(1)} %copy-done), kind=kOutput, calls=%fused_computation.5 | convolution fusion | flops 1075838976 | bytes 8519680 | tf_op jit(solution)/shard_map/dot_general | solution.py:15
  105.9 2.8 gather_fusion
  108.7 7.1 %fusion = f32[16,128,256]{1,2,0:T(8,128)} fusion(f32[8,256]{1,0:T(8,128)S(1)} %convert_element_type.20, bf16[16,128,8,128]{3,2,1,0:T(8,128)(2,1)} %bitcast.66, bf16[16,128,256]{2,1,0:T(8,128)(2,1)S(1)} %gather_fusion), kind=kOutput, calls=%fused_computation.4 | convolution fusion | flops 1081606144 | bytes 7348224 | tf_op jit(solution)/shard_map/cikj,cja->cika/dot_general | solution.py:26
  115.8 2.2 copy.33
  118.0 1.9 fusion.12
  119.9 1.2 copy.34
  121.2 61.4 %all_to_all.5 = f32[16,128,256]{2,1,0:T(8,128)S(1)} all-to-all(f32[16,128,256]{2,1,0:T(8,128)S(1)} %copy.34), channel_id=1, replica_groups=mesh['rows'=32,'cols'=16] {'cols'}, dimensions={0} | all-to-all | bytes 4194304 | tf_op jit(solution)/shard_map/all_to_all | solution.py:33
  182.7 1.1 fusion.21
  183.9 259.9 %all-reduce.3.cloned.1.call-done = f32[256,256]{0,1:T(8,128)} async-done(((f32[256,256]{0,1:T(8,128)}), f32[256,256]{0,1:T(8,128)}) %all-reduce.3.cloned.1.call-update) | async-done | bytes 262160 | tf_op jit(solution)/shard_map/psum | solution.py:36
  443.8 1.1 copy.36
  444.9 1.0 fusion.3
  445.9 11.7 %cholesky.50 = f32[128,128]{1,0:T(8,128)S(1)} custom-call(f32[128,128]{1,0:T(8,128)S(1)} %cholesky.118), custom_call_target="Cholesky" | custom-call | tf_op jit(solution)/shard_map/jit(cholesky)/cholesky | solution.py:37
  457.7 9.8 %custom-call.14 = f32[1,128,128]{1,2,0:T(8,128)S(1)} custom-call(f32[1,128,128]{2,1,0:T(8,128)S(1)} %get-tuple-element.26), custom_call_target="InvertDiagBlocksLowerTriangular" | custom-call | tf_op jit(solution)/shard_map/jit(cholesky)/cholesky | solution.py:37
  468.0 11.7 %cholesky.105 = f32[128,128]{1,0:T(8,128)S(1)} custom-call(f32[128,128]{1,0:T(8,128)S(1)} %convolution_subtract_fusion.1), custom_call_target="Cholesky" | custom-call | tf_op jit(solution)/shard_map/jit(cholesky)/cholesky | solution.py:37
  479.7 0.7 compare_reduce_fusion
  481.8 4.1 while.1
  482.5 1.3 bitcast_dynamic-update-slice_fusion.2
  484.5 1.3 bitcast_dynamic-update-slice_fusion.2
  485.9 19.9 %custom-call.15 = f32[2,128,128]{1,2,0:T(8,128)S(1)} custom-call(f32[2,128,128]{2,1,0:T(8,128)S(1)} %get-tuple-element.12), custom_call_target="InvertDiagBlocksLowerTriangular" | custom-call | tf_op jit(solution)/shard_map/triangular_solve | solution.py:39
  506.6 0.8 copy.38
  (28 shorter events, 3.1 us)
Async XLA Ops:
  6.5 93.9 %copy-start = (bf16[256,256]{1,0:T(8,128)(2,1)S(1)}, bf16[256,256]{1,0:T(8,128)(2,1)}, u32[]{:S(2)}) copy-start(bf16[256,256]{1,0:T(8,128)(2,1)} %param.12) | copy-start | bytes 393220
  6.5 93.9 %all-gather.2.cloned.1.call-start = ((), (), s32[]{:S(2)}) async-start(), calls=%async_computation.1 | async-start | bytes 4325376 | tf_op jit(solution)/shard_map/all_gather | solution.py:16
  7.3 436.5 %all-reduce.3.cloned.1.call-start = ((), (), s32[]{:S(2)}) async-start(), calls=%async_computation.2 | async-start | bytes 524288 | tf_op jit(solution)/shard_map/psum | solution.py:36
Sparse Core Ops, SparseCore 0:
  10.5 89.8 all-gather.1
  183.9 259.8 all-reduce.2
where the time goes:
time: 515 us; the launch traced here: 514 us
  waiting for transfers between devices  351 us (68%)
  blocking collectives  61.4 us (12%)
  other arithmetic  55.9 us (11%)
  matrix products  17.8 us (3%)
  between operations  15.5 us (3%)
  local copies, waits for them, and re-layouts  12.3 us (2%)
    psum x1, waiting for transfers between devices, per_device(): gram_matrix = lax.psum(gram_local, ('rows', 'cols'))  260 us
    all_gather x1, waiting for transfers between devices, per_device(): lax.all_gather(factor_two, 'rows', axis=0, tiled=True)  90.7 us
    all_to_all x1, blocking collectives, per_device(): lax.all_to_all(partials, 'cols', split_axis=0, concat_axis=0, tiled=True)  61.4 us
    another operation x6, other arithmetic, per_device(): chol_factor = jnp.linalg.cholesky(gram_matrix)  34 us
    another operation x3, other arithmetic, per_device(): lax.linalg.triangular_solve(chol_factor, row_sums.T, left_side=True, lowe...  19.9 us
  transfers between devices with their start and end apart: 2, of which 2 were waited for; matrix products, arithmetic and copies ran while one was open for 0% of the time, Pallas kernels for 0%

commit v1 on v0

v1 whole, which is shorter than its diff:
```python
import functools

import jax
import jax.numpy as jnp
from jax import lax
from jax.experimental import pallas as pl
from jax.experimental.pallas import tpu as pltpu
from jax.sharding import PartitionSpec as P

BF = jnp.bfloat16
F32 = jnp.float32
MESH = pl.DeviceIdType.MESH
VMEM = pltpu.VMEM
NX, NY, NZ, NC = 4, 8, 8, 2
MIB = 1024 * 1024

TREE = {
    "y+": [(0, 0), (0, 1), (0, 2), (0, 3), (2, 0), (2, 1), (2, 2), (1, 3)],
    "y-": [(0, 0), (0, -1), (0, -2), (2, 0), (2, -1), (2, -2), (2, -3)],
    "x+": [(0, 0), (0, 1), (1, 0), (0, -1), (0, 3), (0, 2), (0, -2), (0, -3)],
    "x-": [(0, 0), (0, 1), (0, -1), (0, 2), (0, -2), (0, 3), (0, -3), (0, 4)],
}
STEP = {"y+": (0, 1), "y-": (0, -1), "x+": (1, 0), "x-": (-1, 0)}


def place(dx, dy):
    return (dx % NX, dy % NY)


def tree_plan():
    arrival = {}
    plan = []
    for slot in range(8):
        for way in ("y+", "y-", "x+", "x-"):
            if slot < len(TREE[way]):
                edge = len(plan)
                spot = place(*TREE[way][slot])
                plan.append((edge, way, spot))
                to = place(spot[0] + STEP[way][0], spot[1] + STEP[way][1])
                arrival[to] = edge
    return [(e, w, s, arrival.get(s)) for e, w, s in plan], arrival


def gather_kernel(f2_ref, s2_ref, out_ref, send_sem, recv_sem):
    r = lax.axis_index("rows")
    c = lax.axis_index("cols")
    x, y = r // NY, r % NY

    def at(dx, dy):
        return lax.rem(x + (dx % NX), NX) * NY + lax.rem(y + (dy % NY), NY)

    barrier = pltpu.get_barrier_semaphore()
    for dx, dy in STEP.values():
        pl.semaphore_signal(barrier, inc=1, device_id=(at(dx, dy), c), device_id_type=MESH)
    half = f2_ref.shape[0] // 2
    for ch in range(2):
        own = jnp.dot(f2_ref[pl.ds(ch * half, half), :], s2_ref[...], preferred_element_type=F32)
        out_ref[r, ch] = own.astype(BF)
    pl.semaphore_wait(barrier, 4)

    plan, arrival = tree_plan()

    def copy(edge, way, spot, ch):
        src = out_ref.at[at(-spot[0], -spot[1]), ch]
        return pltpu.make_async_remote_copy(
            src_ref=src, dst_ref=src, send_sem=send_sem.at[edge, ch], recv_sem=recv_sem.at[edge, ch],
            device_id=(at(*STEP[way]), c), device_id_type=MESH)

    def wait_arrival(edge, ch):
        _, way, spot, _ = plan[edge]
        to = (spot[0] + STEP[way][0], spot[1] + STEP[way][1])
        dst = out_ref.at[at(-to[0], -to[1]), ch]
        pltpu.make_async_remote_copy(
            src_ref=dst, dst_ref=dst, send_sem=send_sem.at[edge, ch], recv_sem=recv_sem.at[edge, ch],
            device_id=(at(*STEP[way]), c), device_id_type=MESH).wait_recv()

    waited = set()
    slot_of = {}
    n = 0
    for slot in range(8):
        for way in ("y+", "y-", "x+", "x-"):
            if slot < len(TREE[way]):
                slot_of[n] = slot
                n += 1
    for slot in range(8):
        for ch in range(2):
            for edge, way, spot, brought in plan:
                if slot_of[edge] != slot:
                    continue
                if brought is not None and (brought, ch) not in waited:
                    wait_arrival(brought, ch)
                    waited.add((brought, ch))
                copy(edge, way, spot, ch).start()
    for edge, way, spot, brought in plan:
        for ch in range(2):
            if (edge, ch) not in waited:
                wait_arrival(edge, ch)
    for edge, way, spot, brought in plan:
        for ch in range(2):
            copy(edge, way, spot, ch).wait_send()


def gather(f2, s2):
    half, width = f2.shape[0] // 2, s2.shape[1]
    return pl.pallas_call(
        gather_kernel,
        out_shape=jax.ShapeDtypeStruct((NX * NY, 2, half, width), BF),
        in_specs=[pl.BlockSpec(memory_space=VMEM)] * 2,
        out_specs=pl.BlockSpec(memory_space=VMEM),
        scratch_shapes=[pltpu.SemaphoreType.DMA((31, 2)), pltpu.SemaphoreType.DMA((31, 2))],
        compiler_params=pltpu.CompilerParams(collective_id=0, has_side_effects=True, vmem_limit_bytes=16 * MIB),
        name="gather",
    )(f2, s2)


def tiles_kernel(coords, count, tiles_ref, grouped_ref, f3_ref, s3_ref, out_ref):
    size, depth = tiles_ref.shape[1], tiles_ref.shape[2]
    width = s3_ref.shape[1]
    d = jnp.dot(f3_ref[...], s3_ref[...], preferred_element_type=F32).astype(BF).astype(F32)
    out_ref[...] = jnp.zeros_like(out_ref)

    def slot(s, carry):
        q = coords[2 * s + 1]
        p = coords[2 * s]
        xs = tiles_ref[s].reshape(size * depth, tiles_ref.shape[3])
        prod = jnp.dot(xs, grouped_ref[q // 2, lax.rem(q, 2)], preferred_element_type=F32)
        term = jnp.sum(prod.reshape(size, depth, width) * d[None], axis=1)
        out_ref[p] += term
        return carry

    lax.fori_loop(0, count[0], slot, 0)


def tile_products(coords, count, tiles, grouped, f3, s3):
    size = tiles.shape[1]
    width = s3.shape[1]
    return pl.pallas_call(
        tiles_kernel,
        out_shape=jax.ShapeDtypeStruct((NZ * NC, size, width), F32),
        in_specs=[pl.BlockSpec(memory_space=pltpu.SMEM)] * 2 + [pl.BlockSpec(memory_space=VMEM)] * 4,
        out_specs=pl.BlockSpec(memory_space=VMEM),
        compiler_params=pltpu.CompilerParams(vmem_limit_bytes=32 * MIB),
        name="tile_products",
    )(coords, count, tiles, grouped, f3, s3)


def split3(a):
    a1 = a.astype(BF)
    rest = a - a1.astype(F32)
    a2 = rest.astype(BF)
    a3 = (rest - a2.astype(F32)).astype(BF)
    return a1, a2, a3


CHAINS = [(0, -1, 4), (1, 1, 4), (0, 1, 3), (1, -1, 3)]


def reduce_kernel(part_ref, rows_ref, gram_ref, pair_out, pair_in, hop_out, hop_in, mine, own, xin, xsum, yin, ysum, zin,
                  s_pair, r_pair, s_hop, r_hop, s_g, r_g, s_x, r_x, s_y, r_y, s_z, r_z, s_ya, r_ya, s_xa, r_xa, s_pa, r_pa):
    r = lax.axis_index("rows")
    c = lax.axis_index("cols")
    x, y = r // NY, r % NY
    z, core = c // NC, c % NC
    other = 1 - core

    def dev(dx=0, dy=0, dz=0, flip=False):
        row = lax.rem(x + dx, NX) * NY + lax.rem(y + dy, NY)
        return (row, lax.rem(z + dz % NZ, NZ) * NC + (other if flip else core))

    partners = [dev(flip=True)]
    partners += [dev(dx=k) for k in range(1, NX)]
    partners += [dev(dy=k) for k in range(1, NY)]
    partners += [dev(dz=k) for k in range(1, NZ)]
    barrier = pltpu.get_barrier_semaphore()
    for d in partners:
        pl.semaphore_signal(barrier, inc=1, device_id=d, device_id_type=MESH)
    pl.semaphore_wait(barrier, len(partners))

    def copy(src, dst, ssem, rsem, device):
        return pltpu.make_async_remote_copy(src_ref=src, dst_ref=dst, send_sem=ssem, recv_sem=rsem, device_id=device,
                                            device_id_type=MESH)

    order = [4, 3, 5, 2, 6, 1, 7, 0]
    pair = {}
    for d in order:
        pair_out[d] = part_ref[lax.rem(z + d, NZ) * NC + other].astype(BF)
        pair[d] = copy(pair_out.at[d], pair_in.at[d], s_pair.at[d], r_pair.at[d], dev(flip=True))
        pair[d].start()
    ready = set()

    def chip_sum(d, h):
        d = d % NZ
        if d not in ready:
            pair[d].wait_recv()
            ready.add(d)
        cols = pl.ds(h * 128, 128)
        return part_ref[lax.rem(z + d, NZ) * NC + core, :, cols] + pair_in[d, :, cols].astype(F32)

    hops = {}
    for t in range(1, 5):
        for k, (h, way, length) in enumerate(CHAINS):
            if t > length:
                continue
            value = chip_sum(way * (length - t + 1), h)
            if t > 1:
                hops[k, t - 1].wait_recv()
                value = value + hop_in[k, t - 2].astype(F32)
            hop_out[k, t - 1] = value.astype(BF)
            hops[k, t] = copy(hop_out.at[k, t - 1], hop_in.at[k, t - 1], s_hop.at[k, t - 1], r_hop.at[k, t - 1], dev(dz=way))
            hops[k, t].start()
    for h in range(2):
        total = chip_sum(0, h)
        for k, (hh, way, length) in enumerate(CHAINS):
            if hh == h:
                hops[k, length].wait_recv()
                total = total + hop_in[k, length - 1].astype(F32)
        rows_ref[:, pl.ds(h * 128, 128)] = total

    def gram_half(k):
        cols = pl.ds(pl.multiple_of(k * 128, 128), 128)
        return lax.dot_general(rows_ref[...], rows_ref[:, cols], (((0,), (0,)), ((), ())),
                               precision=lax.Precision.HIGHEST, preferred_element_type=F32)

    mine[...] = gram_half(other)
    to_pair = copy(mine, xin.at[0], s_g, r_g, dev(flip=True))
    to_pair.start()
    half = gram_half(core)
    to_pair.wait_recv()
    own[...] = half + xin[0]
    xs = []
    for k in range(1, NX):
        cp = copy(own.at[pl.ds(lax.rem(x + k, NX) * 64, 64), :], xsum.at[k], s_x.at[k], r_x.at[k], dev(dx=k))
        cp.start()
        xs.append(cp)
    acc = own[pl.ds(pl.multiple_of(x * 64, 64), 64), :]
    for k in range(1, NX):
        xs[k - 1].wait_recv()
        acc = acc + xsum[k]
    ysum[...] = acc
    ys = []
    for k in range(1, NY):
        cp = copy(ysum.at[pl.ds(lax.rem(y + k, NY) * 8, 8), :], yin.at[k], s_y.at[k], r_y.at[k], dev(dy=k))
        cp.start()
        ys.append(cp)
    acc = ysum[pl.ds(pl.multiple_of(y * 8, 8), 8), :]
    for k in range(1, NY):
        ys[k - 1].wait_recv()
        acc = acc + yin[k]
    zin[z] = acc
    zs = []
    for k in range(1, NZ):
        cp = copy(zin.at[z], zin.at[z], s_z.at[k], r_z.at[k], dev(dz=k))
        cp.start()
        zs.append(cp)
    for k in range(1, NZ):
        zs[k - 1].wait_recv()
    acc = zin[0]
    for k in range(1, NZ):
        acc = acc + zin[k]
    def piece(xx, yy):
        return gram_ref.at[core, pl.ds(xx * 64 + yy * 8, 8), :]

    gram_ref[core, pl.ds(pl.multiple_of(x * 64 + y * 8, 8), 8), :] = acc
    ya = []
    for k in range(1, NY):
        cp = copy(piece(x, y), piece(x, y), s_ya.at[k], r_ya.at[k], dev(dy=k))
        cp.start()
        ya.append(cp)
    for cp in ya:
        cp.wait_recv()

    def quarter(k):
        return gram_ref.at[core, pl.ds(lax.rem(x + k, NX) * 64, 64), :]

    xa = []
    for k in range(1, NX):
        cp = copy(quarter(0), quarter(0), s_xa.at[k], r_xa.at[k], dev(dx=k))
        cp.start()
        xa.append(cp)
    pa = [copy(quarter(0), quarter(0), s_pa.at[0], r_pa.at[0], dev(flip=True))]
    pa[0].start()
    for k in range(1, NX):
        xa[k - 1].wait_recv()
        cp = copy(quarter(NX - k), quarter(NX - k), s_pa.at[k], r_pa.at[k], dev(flip=True))
        cp.start()
        pa.append(cp)
    for cp in pa:
        cp.wait_recv()
    sends = list(pair.values()) + list(hops.values()) + [to_pair] + xs + ys + zs + ya + xa + pa
    for cp in sends:
        cp.wait_send()


def reduce_all(partials):
    size, width = partials.shape[1:]
    dma = pltpu.SemaphoreType.DMA
    return pl.pallas_call(
        reduce_kernel,
        out_shape=[jax.ShapeDtypeStruct((size, width), F32), jax.ShapeDtypeStruct((2, width, 128), F32)],
        in_specs=[pl.BlockSpec(memory_space=VMEM)],
        out_specs=[pl.BlockSpec(memory_space=VMEM)] * 2,
        scratch_shapes=[
            VMEM((NZ, size, width), BF),
            VMEM((NZ, size, width), BF),
            VMEM((4, 4, size, 128), BF),
            VMEM((4, 4, size, 128), BF),
            VMEM((width, 128), F32),
            VMEM((width, 128), F32),
            VMEM((1, width, 128), F32),
            VMEM((NX, 64, 128), F32),
            VMEM((NY, 8, 128), F32),
            VMEM((64, 128), F32),
            VMEM((NZ, 8, 128), F32),
            dma((NZ,)), dma((NZ,)),
            dma((4, 4)), dma((4, 4)),
            dma, dma,
            dma((NX,)), dma((NX,)),
            dma((NY,)), dma((NY,)),
            dma((NZ,)), dma((NZ,)),
            dma((NY,)), dma((NY,)),
            dma((NX,)), dma((NX,)),
            dma((NX,)), dma((NX,)),
        ],
        compiler_params=pltpu.CompilerParams(collective_id=1, has_side_effects=True, vmem_limit_bytes=24 * MIB),
        name="reduce",
    )(partials)


def eliminate(work, base, size):
    n = work.shape[1]
    blk = work[pl.ds(base, size), :]
    ent = {}
    for k in range(size):
        col = jnp.broadcast_to(blk[:, base + k:base + k + 1], (size, 128))
        for i in range(k, size):
            ent[i, k] = col[i:i + 1, :]
    lane = lax.broadcasted_iota(jnp.int32, (1, n), 1)
    own = (lane >= base) & (lane < base + size)
    rows = []
    for i in range(size):
        rows.append(jnp.where(own, jnp.where(lane == base + i, 1.0, 0.0), blk[i:i + 1, :]))
    reps = n // 128
    for j in range(size):
        inv = 1.0 / ent[j, j]
        mult = {i: ent[i, j] * inv for i in range(j + 1, size)}
        for k in range(j + 1, size):
            for i in range(k, size):
                ent[i, k] = ent[i, k] - mult[i] * ent[k, j]
        for i in range(j + 1, size):
            rows[i] = rows[i] - jnp.concatenate([mult[i]] * reps, axis=1) * rows[j]
        scale = lax.rsqrt(ent[j, j])
        work[pl.ds(base + j, 1), :] = rows[j] * jnp.concatenate([scale] * reps, axis=1)


def inverse_factor(work, size):
    n = work.shape[0]
    for base in range(0, n, size):
        eliminate(work, base, size)
        end = base + size
        if end == n:
            break
        p1, p2, p3 = split3(work[pl.ds(base, size), :])
        rhs = jnp.concatenate([p1, p1, p1, p2, p2, p3], axis=0)
        lhs = jnp.concatenate([p1, p2, p3, p1, p2, p1], axis=0)

        def update(a, b):
            delta = lax.dot_general(lhs[:, a:b], rhs, (((0,), (0,)), ((), ())), preferred_element_type=F32)
            lane = lax.broadcasted_iota(jnp.int32, (b - a, n), 1)
            old = jnp.where((lane >= base) & (lane < end), 0.0, work[pl.ds(a, b - a), :])
            work[pl.ds(a, b - a), :] = old - delta

        update(end, end + size)
        if end + size < n:
            update(end + size, n)
    for base in range(0, n, size):
        lane = lax.broadcasted_iota(jnp.int32, (size, n), 1)
        row = lax.broadcasted_iota(jnp.int32, (size, n), 0) + base
        work[pl.ds(base, size), :] = jnp.where(lane <= row, work[pl.ds(base, size), :], 0.0)


def solve_kernel(scale, gram_ref, rows_ref, out_ref, work):
    work[:, pl.ds(0, 128)] = gram_ref[0]
    work[:, pl.ds(128, 128)] = gram_ref[1]
    inverse_factor(work, 16)
    out = lax.dot_general(rows_ref[...], work[...], (((1,), (1,)), ((), ())), precision=lax.Precision.HIGHEST,
                          preferred_element_type=F32)
    out_ref[...] = out * scale


def solve(gram, rows, scale):
    n = gram.shape[1]
    return pl.pallas_call(
        functools.partial(solve_kernel, scale),
        out_shape=jax.ShapeDtypeStruct(rows.shape, F32),
        in_specs=[pl.BlockSpec(memory_space=VMEM)] * 2,
        out_specs=pl.BlockSpec(memory_space=VMEM),
        scratch_shapes=[VMEM((n, n), F32)],
        compiler_params=pltpu.CompilerParams(vmem_limit_bytes=16 * MIB),
        name="solve",
    )(gram, rows)


def per_device(tiles, tile_coords, tile_counts, factor_two, factor_three, sketch_two, sketch_three):
    grouped = gather(factor_two, sketch_two)
    partials = tile_products(tile_coords.reshape(-1), tile_counts.reshape(-1), tiles[0, 0], grouped, factor_three, sketch_three)
    rows, gram = reduce_all(partials)
    total_rows = rows.shape[0] * lax.axis_size("rows") * lax.axis_size("cols")
    return solve(gram, rows, float(total_rows) ** 0.5)


def solution(mesh):
    return jax.shard_map(
        per_device,
        mesh=mesh,
        in_specs=(
            P("rows", "cols", None, None, None, None),
            P("rows", "cols", None, None),
            P("rows", "cols", None),
            P(("cols", "rows"), None),
            P(),
            P(),
            P(),
        ),
        out_specs=P(("rows", "cols"), None),
        check_vma=False,
    )
```

time: 515 us -> 111 us (0.22)
  waiting for transfers between devices: 351 us -> 0 us
  Pallas kernels: 0 us -> 107 us
  blocking collectives: 61.4 us -> 0 us
  other arithmetic: 55.9 us -> 0 us
  matrix products: 17.8 us -> 0 us
  between operations: 15.5 us -> 0.75 us
  local copies, waits for them, and re-layouts: 12.3 us -> 2.66 us
    psum x1 -> x0, waiting for transfers between devices: 260 us -> none  [per_device(): gram_matrix = lax.psum(gram_local, ('rows', 'cols'))]
    pallas_call x0 -> x4, Pallas kernels: none -> 107 us  [the longest x1 54.5 us: reduce_all(): pl.pallas_call(reduce_kernel, out_shape=[jax.ShapeDtypeStruct((size, widt...]
    all_gather x1 -> x0, waiting for transfers between devices: 90.7 us -> none  [per_device(): lax.all_gather(factor_two, 'rows', axis=0, tiled=True)]
    all_to_all x1 -> x0, blocking collectives: 61.4 us -> none  [per_device(): lax.all_to_all(partials, 'cols', split_axis=0, concat_axis=0, tiled=True)]
    another operation x9 -> x0, other arithmetic: 54 us -> none  [the longest x6 34 us: per_device(): chol_factor = jnp.linalg.cholesky(gram_matrix)]
    dot_general x5 -> x0, matrix products: 16.6 us -> none  [the longest x1 7.1 us: per_device(): jnp.einsum('cikj,cja->cika', slot_tiles, selected, preferred_element_type...]
  transfers between devices with their start and end apart: 2 -> 0, of which waited for: 2 -> 0; matrix products, arithmetic and copies ran while one was open for 0% -> 0% of each run, Pallas kernels for 0% -> 0%
where the time goes in v1:
time: 111 us
  Pallas kernels  107 us (96%)
  local copies, waits for them, and re-layouts  2.66 us (2%)
    pallas_call x1, Pallas kernels, reduce_all(): pl.pallas_call(reduce_kernel, out_shape=[jax.ShapeDtypeStruct((size, widt...  54.5 us
    pallas_call x1, Pallas kernels, gather(): pl.pallas_call(gather_kernel, out_shape=jax.ShapeDtypeStruct((NX * NY, 2,...  33.6 us
    pallas_call x1, Pallas kernels, solve(): pl.pallas_call(functools.partial(solve_kernel, scale), out_shape=jax.Shap...  12.3 us
    pallas_call x1, Pallas kernels, tile_products(): pl.pallas_call(tiles_kernel, out_shape=jax.ShapeDtypeStruct((NZ * NC, siz...  6.78 us
    unnamed x11, local copies, waits for them, and re-layouts  2.57 us

profile of v1, /device:TPU:1, one launch (start us, length us, event | category | flops | bytes accessed | tf_op | source)
XLA Modules:
  0.0 110.6 jit_solution(15068987931980091221)
XLA Ops:
  0.0 0.0 copy-start.1
  0.7 0.8 copy.9
  1.4 0.1 reshape.6.coords
  1.5 0.0 copy-start.2
  1.5 0.9 copy-done.2
  2.4 0.0 copy-start.3
  2.4 0.9 copy-done.3
  3.4 0.0 copy-start
  3.4 0.0 copy-start.4
  3.4 33.6 %gather.1.grouped_ref = bf16[32,2,128,256]{3,2,1,0:T(8,128)(2,1)S(1)} custom-call(bf16[256,256]{1,0:T(8,128)(2,1)S(1)} %copy-done.2, bf16[256,256]{1,0:T(8,128)(2,1)S(1)} %copy-done.3), custom_call_target="tpu_custom_call" | custom-call | tf_op jit(solution)/shard_map/gather/pallas_call | solution.py:105
  36.9 0.0 copy-done.1
  36.9 0.0 copy-done
  36.9 0.0 copy-done.4
  36.9 6.8 %tile_products.1.part_ref = f32[16,128,256]{2,1,0:T(8,128)S(1)} custom-call(s32[32]{0:T(128)S(1)} %reshape.6.coords, s32[1]{0:T(128)} %bitcast.4.count, bf16[16,128,8,128]{3,2,1,0:T(8,128)(2,1)S(1)} %bitcast.5, bf16[32,2,128,256]{3,2,1,0:T(8,128)(2,1)S(1)} %gather.1.grouped_ref, bf16[8,256]{1,0:T(8,128)(2,1)S(1)} %copy-done.4, bf16[256,256]{1,0:T(8,128)(2,1)S(1)} %copy-done.1), custom_call_target="tpu_custom_call" | custom-call | tf_op jit(solution)/shard_map/tile_products/pallas_call | solution.py:137
  43.7 54.5 %reduce.1 = (f32[128,256]{1,0:T(8,128)S(1)}, f32[2,256,128]{2,1,0:T(8,128)S(1)}) custom-call(f32[16,128,256]{2,1,0:T(8,128)S(1)} %tile_products.1.part_ref), custom_call_target="tpu_custom_call" | custom-call | tf_op jit(solution)/shard_map/reduce/pallas_call | solution.py:297
  98.3 12.3 %solve.1 = f32[128,256]{1,0:T(8,128)} custom-call(f32[2,256,128]{2,1,0:T(8,128)S(1)} %get-tuple-element.7.gram_ref, f32[128,256]{1,0:T(8,128)S(1)} %get-tuple-element.8.rows_ref), custom_call_target="tpu_custom_call" | custom-call | tf_op jit(solution)/shard_map/solve/pallas_call | solution.py:392
Async XLA Ops:
  0.0 36.9 %copy-start.1 = (bf16[256,256]{1,0:T(8,128)(2,1)S(1)}, bf16[256,256]{1,0:T(8,128)(2,1)}, u32[]{:S(2)}) copy-start(bf16[256,256]{1,0:T(8,128)(2,1)} %s3_ref.1) | copy-start | bytes 393220
  1.5 0.9 copy-start.2
  2.4 0.9 copy-start.3
  3.4 33.6 %copy-start = (bf16[1,1,16,128,8,128]{5,4,3,2,1,0:T(8,128)(2,1)S(1)}, bf16[1,1,16,128,8,128]{5,4,3,2,1,0:T(8,128)(2,1)}, u32[]{:S(2)}) copy-start(bf16[1,1,16,128,8,128]{5,4,3,2,1,0:T(8,128)(2,1)} %param.7) | copy-start | bytes 12582916
  3.4 33.6 %copy-start.4 = (bf16[8,256]{1,0:T(8,128)(2,1)S(1)}, bf16[8,256]{1,0:T(8,128)(2,1)}, u32[]{:S(2)}) copy-start(bf16[8,256]{1,0:T(8,128)(2,1)} %f3_ref.1) | copy-start | bytes 12292

commit v2 on v0

v2 whole, which is shorter than its diff:
```python
import functools

import jax
import jax.numpy as jnp
from jax import lax
from jax.experimental import pallas as pl
from jax.experimental.pallas import tpu as pltpu
from jax.sharding import PartitionSpec as P

BF = jnp.bfloat16
F32 = jnp.float32
MESH = pl.DeviceIdType.MESH
VMEM = pltpu.VMEM
NX, NY, NZ, NC = 4, 8, 8, 2
MIB = 1024 * 1024

TREE = {
    "y+": [(0, 0), (0, 1), (0, 2), (0, 3), (2, 0), (2, 1), (2, 2), (1, 3)],
    "y-": [(0, 0), (0, -1), (0, -2), (2, 0), (2, -1), (2, -2), (2, -3)],
    "x+": [(0, 0), (0, 1), (1, 0), (0, -1), (0, 3), (0, 2), (0, -2), (0, -3)],
    "x-": [(0, 0), (0, 1), (0, -1), (0, 2), (0, -2), (0, 3), (0, -3), (0, 4)],
}
STEP = {"y+": (0, 1), "y-": (0, -1), "x+": (1, 0), "x-": (-1, 0)}


def place(dx, dy):
    return (dx % NX, dy % NY)


def tree_plan():
    arrival = {}
    plan = []
    for slot in range(8):
        for way in ("y+", "y-", "x+", "x-"):
            if slot < len(TREE[way]):
                edge = len(plan)
                spot = place(*TREE[way][slot])
                plan.append((edge, way, spot))
                to = place(spot[0] + STEP[way][0], spot[1] + STEP[way][1])
                arrival[to] = edge
    return [(e, w, s, arrival.get(s)) for e, w, s in plan], arrival


PARTS = 4


def gather_rows(geo, grouped, send_sem, recv_sem, between):
    x, y, c = geo

    def at(dx, dy):
        return lax.rem(x + (dx % NX), NX) * NY + lax.rem(y + (dy % NY), NY)

    plan, _ = tree_plan()

    def copy(edge, way, spot, ch):
        piece = grouped.at[2 * at(-spot[0], -spot[1]) + ch // 2, ch % 2]
        return pltpu.make_async_remote_copy(
            src_ref=piece, dst_ref=piece, send_sem=send_sem.at[edge, ch], recv_sem=recv_sem.at[edge, ch],
            device_id=(at(*STEP[way]), c), device_id_type=MESH)

    def wait_arrival(edge, ch):
        _, way, spot, _ = plan[edge]
        copy(edge, way, (spot[0] + STEP[way][0], spot[1] + STEP[way][1]), ch).wait_recv()

    waited = set()
    started = []
    by_slot = [[e for e in plan if slot_at(e) == slot] for slot in range(8)]
    step = 0
    for slot in range(8):
        for ch in range(PARTS):
            for edge, way, spot, brought in by_slot[slot]:
                if brought is not None and (brought, ch) not in waited:
                    wait_arrival(brought, ch)
                    waited.add((brought, ch))
                started.append(copy(edge, way, spot, ch))
                started[-1].start()
            between[step]()
            step += 1
    for ch in range(PARTS):
        for edge, way, spot, brought in plan:
            if (edge, ch) not in waited:
                wait_arrival(edge, ch)
    return started


def slot_at(entry):
    return [place(*p) for p in TREE[entry[1]]].index(entry[2])


def split3(a):
    a1 = a.astype(BF)
    rest = a - a1.astype(F32)
    a2 = rest.astype(BF)
    a3 = (rest - a2.astype(F32)).astype(BF)
    return a1, a2, a3


CUTS = 2
CHAINS = [(0, -1, 4), (1, 1, 4), (0, 1, 3), (1, -1, 3)]


def rows_kernel(coords_hbm, count_hbm, tiles_hbm, f2_hbm, s2_hbm, f3_hbm, s3_hbm, rows_ref, gram_ref,
                f2_ref, s2_ref, f3_ref, s3_ref, raw, tiles_ref, grouped, flat, terms, sums_ref, coords, count, table,
                pair_out, pair_in, hop_out, hop_in, mine, own, xin, plane_in, zin,
                l_sem, t_sem, s_gather, r_gather,
                s_pair, r_pair, s_hop, r_hop, s_g, r_g, s_x, r_x, s_z, r_z, s_y, r_y, s_pa, r_pa):
    r = lax.axis_index("rows")
    c = lax.axis_index("cols")
    x, y = r // NY, r % NY
    z, core = c // NC, c % NC
    other = 1 - core
    slots, size, depth = raw.shape[0], raw.shape[1], raw.shape[2]

    def dev(dx=0, dy=0, dz=0, flip=False):
        row = lax.rem(x + dx, NX) * NY + lax.rem(y + dy, NY)
        return (row, lax.rem(z + dz % NZ, NZ) * NC + (other if flip else core))

    def copy(src, dst, ssem, rsem, device):
        return pltpu.make_async_remote_copy(src_ref=src, dst_ref=dst, send_sem=ssem, recv_sem=rsem, device_id=device,
                                            device_id_type=MESH)

    partners = [dev(flip=True), dev(dx=1), dev(dx=NX - 1), dev(dy=1), dev(dy=NY - 1), dev(dz=1), dev(dz=-1)]
    barrier = pltpu.get_barrier_semaphore()
    for d in partners:
        pl.semaphore_signal(barrier, inc=1, device_id=d, device_id_type=MESH)
    local = [pltpu.make_async_copy(src, dst, l_sem.at[i]) for i, (src, dst) in enumerate(
        [(f2_hbm, f2_ref), (s2_hbm, s2_ref), (coords_hbm, coords), (count_hbm, count),
         (f3_hbm, f3_ref), (s3_hbm, s3_ref)])]
    fetch = [pltpu.make_async_copy(tiles_hbm.at[s], raw.at[s], t_sem.at[s]) for s in range(slots)]
    for cp in local + fetch:
        cp.start()
    local[0].wait()
    local[1].wait()
    block = jnp.dot(f2_ref[...], s2_ref[...], preferred_element_type=F32).astype(BF)
    grouped[pl.ds(2 * r, 2)] = block.reshape((2,) + grouped.shape[1:])
    pl.semaphore_wait(barrier, len(partners))

    def order_slots():
        local[2].wait()
        local[3].wait()
        live = count[0, 0, 0]
        key = [jnp.where(s < live, coords[0, s], NZ * NC) for s in range(slots)]
        rank = []
        for s in range(slots):
            before = jnp.int32(0)
            for t in range(slots):
                if t < s:
                    before += jnp.where(key[t] <= key[s], 1, 0)
                elif t > s:
                    before += jnp.where(key[t] < key[s], 1, 0)
            rank.append(before)
        last = jnp.int32(-1)
        for k in range(slots):
            who, here = jnp.int32(0), jnp.int32(0)
            for s in range(slots):
                hit = rank[s] == k
                who += jnp.where(hit, s, 0)
                here += jnp.where(hit, key[s], 0)
            table[0, k] = who
            table[1, k] = jnp.where(here == last, 1, 0)
            last = here
        below = jnp.int32(0)
        for b in range(NZ * NC):
            upto = jnp.int32(0)
            for s in range(slots):
                upto += jnp.where(key[s] <= b, 1, 0)
            table[2, b] = jnp.maximum(upto - 1, 0)
            table[3, b] = jnp.where(upto > below, 1, 0)
            below = upto

    part = size // 2

    def reorder(i):
        s, h = i // 2, i % 2
        if h == 0:
            fetch[s].wait()
        rows = raw[s, pl.ds(h * part, part)].astype(F32)
        flat[h] = rows.reshape(part * depth, rows.shape[2])
        for k in range(depth):
            tiles_ref[s, pl.ds(k * size + h * part, part), :] = flat[h, pl.ds(k, part, stride=depth), :].astype(BF)

    between = [lambda: None] * (8 * PARTS)
    todo = 2 * slots
    for i in range(todo):
        at = min(2 + i, 8 * PARTS - 1)
        between[at] = (lambda f, i=i: (lambda: (f(), reorder(i))))(between[at])
    between[1] = order_slots
    gathers = gather_rows((x, y, c), grouped, s_gather, r_gather, between)

    local[4].wait()
    local[5].wait()
    weight = jnp.dot(f3_ref[...], s3_ref[...], preferred_element_type=F32).astype(BF).astype(F32)
    for s in range(slots):
        sel = grouped[coords[1, s]].reshape(size, weight.shape[1])
        term = None
        for k in range(depth):
            prod = jnp.dot(tiles_ref[s, pl.ds(k * size, size), :], sel, preferred_element_type=F32) * weight[k:k + 1, :]
            term = prod if term is None else term + prod
        terms[s] = term
    total = None
    for k in range(slots):
        total = terms[table[0, k]] if k == 0 else jnp.where(table[1, k] == 1, total, 0.0) + terms[table[0, k]]
        sums_ref[k] = total

    def partial_rows(b, cols, rows):
        return jnp.where(table[3, b] == 1, sums_ref[table[2, b], rows, cols], 0.0)

    every, whole = pl.ds(0, size), pl.ds(0, weight.shape[1])

    order = [4, 3, 5, 2, 6, 1, 7, 0]
    pair = {}
    for d in order:
        pair_out[d] = partial_rows(lax.rem(z + d, NZ) * NC + other, whole, every).astype(BF)
        pair[d] = copy(pair_out.at[d], pair_in.at[d], s_pair.at[d], r_pair.at[d], dev(flip=True))
        pair[d].start()
    ready = set()

    def chip_sum(d, h, u):
        d = d % NZ
        if d not in ready:
            pair[d].wait_recv()
            ready.add(d)
        rows, cols = pl.ds(u * cut, cut), pl.ds(h * 128, 128)
        return partial_rows(lax.rem(z + d, NZ) * NC + core, cols, rows) + pair_in[d, rows, cols].astype(F32)

    cut = size // CUTS
    hops = {}
    for t in range(1, 5):
        for u in range(CUTS):
            rows = pl.ds(u * cut, cut)
            for k, (h, way, length) in enumerate(CHAINS):
                if t > length:
                    continue
                value = chip_sum(way * (length - t + 1), h, u)
                if t > 1:
                    hops[k, t - 1, u].wait_recv()
                    value = value + hop_in[k, t - 2, rows].astype(F32)
                hop_out[k, t - 1, rows] = value.astype(BF)
                hops[k, t, u] = copy(hop_out.at[k, t - 1, rows], hop_in.at[k, t - 1, rows],
                                     s_hop.at[k, t - 1, u], r_hop.at[k, t - 1, u], dev(dz=way))
                hops[k, t, u].start()
    for u in range(CUTS):
        rows = pl.ds(u * cut, cut)
        for h in range(2):
            total = chip_sum(0, h, u)
            for k, (hh, way, length) in sorted(enumerate(CHAINS), key=lambda v: v[1][2]):
                if hh == h:
                    hops[k, length, u].wait_recv()
                    total = total + hop_in[k, length - 1, rows].astype(F32)
            rows_ref[rows, pl.ds(h * 128, 128)] = total

    def gram_half(k):
        cols = pl.ds(pl.multiple_of(k * 128, 128), 128)
        return lax.dot_general(rows_ref[...], rows_ref[:, cols], (((0,), (0,)), ((), ())),
                               precision=lax.Precision.HIGHEST, preferred_element_type=F32)

    mine[...] = gram_half(other)
    to_pair = copy(mine, xin.at[0], s_g, r_g, dev(flip=True))
    to_pair.start()
    half = gram_half(core)
    to_pair.wait_recv()
    own[...] = half + xin[0]
    far_x, far_y = (2, 1, 3, 0), (4, 3, 5, 2, 6, 1, 7, 0)
    reach = [(dx, dy) for dx in far_x for dy in far_y if (dx, dy) != (0, 0)]

    def piece(ref, dx, dy):
        row = (lax.rem(x + dx % NX, NX) * NY + lax.rem(y + dy % NY, NY)) * 8
        return ref.at[pl.ds(pl.multiple_of(row, 8), 8), :]

    spread = {}
    for dx, dy in reach:
        spread[dx, dy] = copy(piece(own, dx, dy), plane_in.at[dx, dy], s_x.at[dx, dy], r_x.at[dx, dy], dev(dx=dx, dy=dy))
        spread[dx, dy].start()
    acc = piece(own, 0, 0)[...]
    for dx, dy in reversed(reach):
        spread[dx, dy].wait_recv()
        acc = acc + plane_in[dx, dy]
    zin[z] = acc
    zs = []
    for k in (4, 3, 5, 2, 6, 1, 7):
        cp = copy(zin.at[z], zin.at[z], s_z.at[k], r_z.at[k], dev(dz=k))
        cp.start()
        zs.append(cp)
    for cp in zs:
        cp.wait_recv()
    acc = zin[0]
    for k in range(1, NZ):
        acc = acc + zin[k]
    half_ref = gram_ref.at[core]
    piece(half_ref, 0, 0)[...] = acc
    back = {}
    for dx, dy in reach:
        back[dx, dy] = copy(piece(half_ref, 0, 0), piece(half_ref, 0, 0), s_y.at[dx, dy], r_y.at[dx, dy], dev(dx=dx, dy=dy))
        back[dx, dy].start()
    pa = []
    for dx in reversed(far_x):
        for dy in reversed(far_y):
            if (dx, dy) != (0, 0):
                back[dx, dy].wait_recv()
        quarter = half_ref.at[pl.ds(pl.multiple_of(lax.rem(x + (NX - dx), NX) * 64, 64), 64), :]
        cp = copy(quarter, quarter, s_pa.at[dx], r_pa.at[dx], dev(flip=True))
        cp.start()
        pa.append(cp)
    for cp in pa:
        cp.wait_recv()
    sends = gathers + list(pair.values()) + list(hops.values()) + [to_pair] + list(spread.values()) + zs + list(back.values()) + pa
    for cp in sends:
        cp.wait_send()


def new_rows(coords, count, tiles, f2, f3, s2, s3):
    slots, size, depth, inner = tiles.shape
    width = s2.shape[1]
    dma = pltpu.SemaphoreType.DMA
    hbm = pl.BlockSpec(memory_space=pltpu.HBM)
    return pl.pallas_call(
        rows_kernel,
        out_shape=[jax.ShapeDtypeStruct((size, width), F32), jax.ShapeDtypeStruct((2, width, 128), F32)],
        in_specs=[hbm] * 7,
        out_specs=[pl.BlockSpec(memory_space=VMEM)] * 2,
        scratch_shapes=[
            VMEM(f2.shape, BF),
            VMEM(s2.shape, BF),
            VMEM(f3.shape, BF),
            VMEM(s3.shape, BF),
            VMEM(tiles.shape, BF),
            VMEM((slots, depth * size, inner), BF),
            VMEM((2 * NX * NY, 2, f2.shape[0] // PARTS, width), BF),
            VMEM((2, size * depth // 2, inner), F32),
            VMEM((slots, size, width), F32),
            VMEM((slots, size, width), F32),
            pltpu.SMEM(coords.shape, jnp.int32),
            pltpu.SMEM(count.shape, jnp.int32),
            pltpu.SMEM((4, slots), jnp.int32),
            VMEM((NZ, size, width), BF),
            VMEM((NZ, size, width), BF),
            VMEM((4, 4, size, 128), BF),
            VMEM((4, 4, size, 128), BF),
            VMEM((width, 128), F32),
            VMEM((width, 128), F32),
            VMEM((1, width, 128), F32),
            VMEM((NX, NY, 8, 128), F32),
            VMEM((NZ, 8, 128), F32),
            dma((6,)), dma((slots,)),
            dma((31, PARTS)), dma((31, PARTS)),
            dma((NZ,)), dma((NZ,)),
            dma((4, 4, CUTS)), dma((4, 4, CUTS)),
            dma, dma,
            dma((NX, NY)), dma((NX, NY)),
            dma((NZ,)), dma((NZ,)),
            dma((NX, NY)), dma((NX, NY)),
            dma((NX,)), dma((NX,)),
        ],
        compiler_params=pltpu.CompilerParams(collective_id=0, has_side_effects=True, vmem_limit_bytes=63 * MIB),
        name="new_rows",
    )(coords, count, tiles, f2, s2, f3, s3)


def eliminate(work, base, size, sub):
    n = work.shape[1]
    row = lax.broadcasted_iota(jnp.int32, (sub, 128), 0)
    lane = lax.broadcasted_iota(jnp.int32, (sub, 128), 1)
    parts, groups = size // sub, n // 128
    home, off = base // 128, base % 128
    panel = [[work[pl.ds(base + c * sub, sub), pl.ds(g * 128, 128)] for c in range(parts)] for g in range(groups)]
    block = list(panel[home])
    for c in range(parts):
        unit = jnp.where(lane == off + c * sub + row, 1.0, 0.0)
        panel[home][c] = jnp.where((lane >= off) & (lane < off + size), unit, block[c])
    diag = [None] * parts

    def spread(v, j):
        return jnp.broadcast_to(v[j:j + 1, :], (sub, 128))

    for s in range(parts):
        below = range(s, parts)
        first = off + s * sub
        cols = {c: [jnp.broadcast_to(block[c][:, first + k:first + k + 1], (sub, 128)) for k in range(sub)] for c in below}
        diag[s] = jnp.ones((sub, 128), F32)
        for j in range(sub):
            pivot = spread(cols[s][j], j)
            inv = 1.0 / pivot
            mult = {c: cols[c][j] * inv for c in below}
            mult[s] = jnp.where(row > j, mult[s], 0.0)
            diag[s] = jnp.where(row == j, pivot, diag[s])
            for k in range(j + 1, sub):
                top = spread(cols[s][k], j)
                for c in below:
                    cols[c][k] = cols[c][k] - mult[c] * top
            for g in panel + ([block] if s < parts - 1 else []):
                top = spread(g[s], j)
                for c in below:
                    g[c] = g[c] - mult[c] * top
    for c in range(parts):
        scale = lax.rsqrt(diag[c])
        for g in range(groups):
            work[pl.ds(base + c * sub, sub), pl.ds(g * 128, 128)] = panel[g][c] * scale


def inverse_factor(work, size):
    n = work.shape[0]
    for base in range(0, n, size):
        eliminate(work, base, size, 16)
        end = base + size
        if end == n:
            break
        p1, p2, p3 = split3(work[pl.ds(base, size), :])
        rhs = jnp.concatenate([p1, p1, p1, p2, p2, p3], axis=0)
        lhs = jnp.concatenate([p1, p2, p3, p1, p2, p1], axis=0)

        def update(a, b):
            delta = lax.dot_general(lhs[:, a:b], rhs, (((0,), (0,)), ((), ())), preferred_element_type=F32)
            lane = lax.broadcasted_iota(jnp.int32, (b - a, n), 1)
            old = jnp.where((lane >= base) & (lane < end), 0.0, work[pl.ds(a, b - a), :])
            work[pl.ds(a, b - a), :] = old - delta

        update(end, end + size)
        if end + size < n:
            update(end + size, n)
    for base in range(0, n, size):
        lane = lax.broadcasted_iota(jnp.int32, (size, n), 1)
        row = lax.broadcasted_iota(jnp.int32, (size, n), 0) + base
        work[pl.ds(base, size), :] = jnp.where(lane <= row, work[pl.ds(base, size), :], 0.0)


def solve_kernel(scale, gram_hbm, rows_hbm, out_ref, work, rows, sem):
    copies = [pltpu.make_async_copy(gram_hbm.at[h], work.at[:, pl.ds(h * 128, 128)], sem.at[h]) for h in range(2)]
    copies.append(pltpu.make_async_copy(rows_hbm, rows, sem.at[2]))
    for cp in copies:
        cp.start()
    copies[0].wait()
    copies[1].wait()
    inverse_factor(work, 32)
    copies[2].wait()
    out = lax.dot_general(rows[...], work[...], (((1,), (1,)), ((), ())), precision=lax.Precision.HIGHEST,
                          preferred_element_type=F32)
    out_ref[...] = out * scale


def solve(gram, rows, scale):
    n = gram.shape[1]
    return pl.pallas_call(
        functools.partial(solve_kernel, scale),
        out_shape=jax.ShapeDtypeStruct(rows.shape, F32),
        in_specs=[pl.BlockSpec(memory_space=pltpu.HBM)] * 2,
        out_specs=pl.BlockSpec(memory_space=VMEM),
        scratch_shapes=[VMEM((n, n), F32), VMEM(rows.shape, F32), pltpu.SemaphoreType.DMA((3,))],
        compiler_params=pltpu.CompilerParams(vmem_limit_bytes=63 * MIB),
        name="solve",
    )(gram, rows)


def per_device(tiles, tile_coords, tile_counts, factor_two, factor_three, sketch_two, sketch_three):
    rows, gram = new_rows(tile_coords[0, 0].T, tile_counts, tiles[0, 0], factor_two, factor_three, sketch_two, sketch_three)
    total_rows = rows.shape[0] * lax.axis_size("rows") * lax.axis_size("cols")
    return solve(gram, rows, float(total_rows) ** 0.5)


def solution(mesh):
    return jax.shard_map(
        per_device,
        mesh=mesh,
        in_specs=(
            P("rows", "cols", None, None, None, None),
            P("rows", "cols", None, None),
            P("rows", "cols", None),
            P(("cols", "rows"), None),
            P(),
            P(),
            P(),
        ),
        out_specs=P(("rows", "cols"), None),
        check_vma=False,
    )
```

time: 515 us -> 92.9 us (0.18)
  waiting for transfers between devices: 351 us -> 0 us
  Pallas kernels: 0 us -> 91.9 us
  blocking collectives: 61.4 us -> 0 us
  other arithmetic: 55.9 us -> 0 us
  matrix products: 17.8 us -> 0 us
  between operations: 15.5 us -> 0.82 us
  local copies, waits for them, and re-layouts: 12.3 us -> 0 us
    psum x1 -> x0, waiting for transfers between devices: 260 us -> none  [per_device(): gram_matrix = lax.psum(gram_local, ('rows', 'cols'))]
    pallas_call x0 -> x2, Pallas kernels: none -> 91.9 us  [the longest x1 83.1 us: new_rows(): pl.pallas_call(rows_kernel, out_shape=[jax.ShapeDtypeStruct((size, width)...]
    all_gather x1 -> x0, waiting for transfers between devices: 90.7 us -> none  [per_device(): lax.all_gather(factor_two, 'rows', axis=0, tiled=True)]
    all_to_all x1 -> x0, blocking collectives: 61.4 us -> none  [per_device(): lax.all_to_all(partials, 'cols', split_axis=0, concat_axis=0, tiled=True)]
    another operation x9 -> x0, other arithmetic: 54 us -> none  [the longest x6 34 us: per_device(): chol_factor = jnp.linalg.cholesky(gram_matrix)]
    dot_general x5 -> x0, matrix products: 16.6 us -> none  [the longest x1 7.1 us: per_device(): jnp.einsum('cikj,cja->cika', slot_tiles, selected, preferred_element_type...]
  transfers between devices with their start and end apart: 2 -> 0, of which waited for: 2 -> 0; matrix products, arithmetic and copies ran while one was open for 0% -> 0% of each run, Pallas kernels for 0% -> 0%
where the time goes in v2:
time: 92.9 us; the launch traced here: 92.7 us
  Pallas kernels  91.9 us (99%)
    pallas_call x1, Pallas kernels, new_rows(): pl.pallas_call(rows_kernel, out_shape=[jax.ShapeDtypeStruct((size, width)...  83.1 us
    pallas_call x1, Pallas kernels, solve(): pl.pallas_call(functools.partial(solve_kernel, scale), out_shape=jax.Shap...  8.79 us

profile of v2, /device:TPU:1, one launch (start us, length us, event | category | flops | bytes accessed | tf_op | source)
XLA Modules:
  0.0 92.7 jit_solution(5248328769339765187)
XLA Ops:
  0.7 83.1 %new_rows.1 = (f32[128,256]{1,0:T(8,128)}, f32[2,256,128]{2,1,0:T(8,128)}) custom-call(s32[2,16]{1,0:T(2,128)} %bitcast.5, s32[1,1,1]{2,1,0:T(1,128)S(6)} %copy.8.count_hbm, bf16[16,128,8,128]{3,2,1,0:T(8,128)(2,1)} %bitcast.4, bf16[256,256]{1,0:T(8,128)(2,1)} %f2_hbm.1, bf16[256,256]{1,0:T(8,128)(2,1)} %s2_hbm.1, bf16[8,256]{1,0:T(8,128)(2,1)} %f3_hbm.1, ...), custom_call_target="tpu_custom_call" | custom-call | tf_op jit(solution)/shard_map/new_rows/pallas_call | solution.py:316
  83.8 8.8 %solve.1 = f32[128,256]{1,0:T(8,128)} custom-call(f32[2,256,128]{2,1,0:T(8,128)} %get-tuple-element.7.gram_hbm, f32[128,256]{1,0:T(8,128)} %get-tuple-element.8.rows_hbm), custom_call_target="tpu_custom_call" | custom-call | tf_op jit(solution)/shard_map/solve/pallas_call | solution.py:442

commit v3 on v2

--- a/solution.py
+++ b/solution.py
@@ -14,34 +14,44 @@
 NX, NY, NZ, NC = 4, 8, 8, 2
 MIB = 1024 * 1024
 
+PARTS = 4
+
 TREE = {
-    "y+": [(0, 0), (0, 1), (0, 2), (0, 3), (2, 0), (2, 1), (2, 2), (1, 3)],
-    "y-": [(0, 0), (0, -1), (0, -2), (2, 0), (2, -1), (2, -2), (2, -3)],
-    "x+": [(0, 0), (0, 1), (1, 0), (0, -1), (0, 3), (0, 2), (0, -2), (0, -3)],
+    "y+": [(0, 0), (0, 1), (0, 2), (2, 0), (0, 3), (2, 1), (1, 3), (2, 2)],
+    "y-": [(0, 0), (0, -1), (2, 0), (0, -2), (2, -1), (2, -2), (2, -3)],
+    "x+": [(0, 0), (1, 0), (0, 1), (0, -1), (0, 3), (0, 2), (0, -2), (0, -3)],
     "x-": [(0, 0), (0, 1), (0, -1), (0, 2), (0, -2), (0, 3), (0, -3), (0, 4)],
 }
 STEP = {"y+": (0, 1), "y-": (0, -1), "x+": (1, 0), "x-": (-1, 0)}
+FLIP = {"y+": "y-", "y-": "y+", "x+": "x-", "x-": "x+"}
 
 
 def place(dx, dy):
     return (dx % NX, dy % NY)
 
 
+def trees():
+    first = {w: [place(*s) for s in spots] for w, spots in TREE.items()}
+    second = {(FLIP[w] if w[0] == "y" else w): [place(a, -b) for a, b in spots] for w, spots in first.items()}
+    third = {w: list(spots) for w, spots in first.items()}
+    third["x-"].remove(place(0, -3))
+    third["y-"].append(place(-1, -2))
+    fourth = {(FLIP[w] if w[0] == "x" else w): [place(-a, b) for a, b in spots] for w, spots in third.items()}
+    return [first, second, third, fourth]
+
+
 def tree_plan():
-    arrival = {}
-    plan = []
-    for slot in range(8):
-        for way in ("y+", "y-", "x+", "x-"):
-            if slot < len(TREE[way]):
-                edge = len(plan)
-                spot = place(*TREE[way][slot])
-                plan.append((edge, way, spot))
-                to = place(spot[0] + STEP[way][0], spot[1] + STEP[way][1])
-                arrival[to] = edge
-    return [(e, w, s, arrival.get(s)) for e, w, s in plan], arrival
-
-
-PARTS = 4
+    plans = []
+    for tree in trees():
+        arrival, plan = {}, []
+        for slot in range(8):
+            for way in STEP:
+                if slot < len(tree[way]):
+                    spot = tree[way][slot]
+                    arrival[place(spot[0] + STEP[way][0], spot[1] + STEP[way][1])] = len(plan)
+                    plan.append((len(plan), slot, way, spot))
+        plans.append([entry + (arrival.get(entry[3]),) for entry in plan])
+    return plans
 
 
 def gather_rows(geo, grouped, send_sem, recv_sem, between):
@@ -50,41 +60,38 @@
     def at(dx, dy):
         return lax.rem(x + (dx % NX), NX) * NY + lax.rem(y + (dy % NY), NY)
 
-    plan, _ = tree_plan()
-
-    def copy(edge, way, spot, ch):
-        piece = grouped.at[2 * at(-spot[0], -spot[1]) + ch // 2, ch % 2]
+    plans = [tree_plan()[ch % 4] for ch in range(PARTS)]
+
+    def copy(ch, edge, way, spot):
+        piece = grouped.at[2 * at(-spot[0], -spot[1]) + ch // (PARTS // 2), ch % (PARTS // 2)]
         return pltpu.make_async_remote_copy(
             src_ref=piece, dst_ref=piece, send_sem=send_sem.at[edge, ch], recv_sem=recv_sem.at[edge, ch],
             device_id=(at(*STEP[way]), c), device_id_type=MESH)
 
-    def wait_arrival(edge, ch):
-        _, way, spot, _ = plan[edge]
-        copy(edge, way, (spot[0] + STEP[way][0], spot[1] + STEP[way][1]), ch).wait_recv()
+    def wait_arrival(ch, edge):
+        _, _, way, spot, _ = plans[ch][edge]
+        copy(ch, edge, way, place(spot[0] + STEP[way][0], spot[1] + STEP[way][1])).wait_recv()
 
     waited = set()
     started = []
-    by_slot = [[e for e in plan if slot_at(e) == slot] for slot in range(8)]
     step = 0
-    for slot in range(8):
+    for now in range(8):
         for ch in range(PARTS):
-            for edge, way, spot, brought in by_slot[slot]:
-                if brought is not None and (brought, ch) not in waited:
-                    wait_arrival(brought, ch)
-                    waited.add((brought, ch))
-                started.append(copy(edge, way, spot, ch))
+            for edge, slot, way, spot, brought in plans[ch]:
+                if slot != now:
+                    continue
+                if brought is not None and (ch, brought) not in waited:
+                    wait_arrival(ch, brought)
+                    waited.add((ch, brought))
+                started.append(copy(ch, edge, way, spot))
                 started[-1].start()
             between[step]()
             step += 1
     for ch in range(PARTS):
-        for edge, way, spot, brought in plan:
-            if (edge, ch) not in waited:
-                wait_arrival(edge, ch)
+        for entry in plans[ch]:
+            if (ch, entry[0]) not in waited:
+                wait_arrival(ch, entry[0])
     return started
-
-
-def slot_at(entry):
-    return [place(*p) for p in TREE[entry[1]]].index(entry[2])
 
 
 def split3(a):
@@ -99,9 +106,9 @@
 CHAINS = [(0, -1, 4), (1, 1, 4), (0, 1, 3), (1, -1, 3)]
 
 
-def rows_kernel(coords_hbm, count_hbm, tiles_hbm, f2_hbm, s2_hbm, f3_hbm, s3_hbm, rows_ref, gram_ref,
-                f2_ref, s2_ref, f3_ref, s3_ref, raw, tiles_ref, grouped, flat, terms, sums_ref, coords, count, table,
-                pair_out, pair_in, hop_out, hop_in, mine, own, xin, plane_in, zin,
+def rows_kernel(scale, coords_hbm, count_hbm, tiles_hbm, f2_hbm, s2_hbm, f3_hbm, s3_hbm, out_ref,
+                rows_ref, gram_ref, work, f2_ref, s2_ref, f3_ref, s3_ref, raw, tiles_ref, grouped, flat, terms, sums_ref, coords, count, table,
+                pair_out, pair_in, hop_out, hop_in, rows_in, own, plane_in, zin,
                 l_sem, t_sem, s_gather, r_gather,
                 s_pair, r_pair, s_hop, r_hop, s_g, r_g, s_x, r_x, s_z, r_z, s_y, r_y, s_pa, r_pa):
     r = lax.axis_index("rows")
@@ -239,6 +246,7 @@
                 hops[k, t, u] = copy(hop_out.at[k, t - 1, rows], hop_in.at[k, t - 1, rows],
                                      s_hop.at[k, t - 1, u], r_hop.at[k, t - 1, u], dev(dz=way))
                 hops[k, t, u].start()
+    swap = []
     for u in range(CUTS):
         rows = pl.ds(u * cut, cut)
         for h in range(2):
@@ -248,18 +256,18 @@
                     hops[k, length, u].wait_recv()
                     total = total + hop_in[k, length - 1, rows].astype(F32)
             rows_ref[rows, pl.ds(h * 128, 128)] = total
-
-    def gram_half(k):
-        cols = pl.ds(pl.multiple_of(k * 128, 128), 128)
-        return lax.dot_general(rows_ref[...], rows_ref[:, cols], (((0,), (0,)), ((), ())),
+        swap.append(copy(rows_ref.at[rows], rows_in.at[rows], s_g.at[u], r_g.at[u], dev(flip=True)))
+        swap[-1].start()
+
+    def gram_half(ref):
+        cols = pl.ds(pl.multiple_of(core * 128, 128), 128)
+        return lax.dot_general(ref[...], ref[:, cols], (((0,), (0,)), ((), ())),
                                precision=lax.Precision.HIGHEST, preferred_element_type=F32)
 
-    mine[...] = gram_half(other)
-    to_pair = copy(mine, xin.at[0], s_g, r_g, dev(flip=True))
-    to_pair.start()
-    half = gram_half(core)
-    to_pair.wait_recv()
-    own[...] = half + xin[0]
+    half = gram_half(rows_ref)
+    for cp in swap:
+        cp.wait_recv()
+    own[...] = half + gram_half(rows_in)
     far_x, far_y = (2, 1, 3, 0), (4, 3, 5, 2, 6, 1, 7, 0)
     reach = [(dx, dy) for dx in far_x for dy in far_y if (dx, dy) != (0, 0)]
 
@@ -303,29 +311,38 @@
         pa.append(cp)
     for cp in pa:
         cp.wait_recv()
-    sends = gathers + list(pair.values()) + list(hops.values()) + [to_pair] + list(spread.values()) + zs + list(back.values()) + pa
+    for h in range(2):
+        work[:, pl.ds(h * 128, 128)] = gram_ref[h]
+    inverse_factor(work, 32)
+    out = lax.dot_general(rows_ref[...], work[...], (((1,), (1,)), ((), ())), precision=lax.Precision.HIGHEST,
+                          preferred_element_type=F32)
+    out_ref[...] = out * scale
+    sends = gathers + list(pair.values()) + list(hops.values()) + swap + list(spread.values()) + zs + list(back.values()) + pa
     for cp in sends:
         cp.wait_send()
 
 
-def new_rows(coords, count, tiles, f2, f3, s2, s3):
+def new_factor(scale, coords, count, tiles, f2, f3, s2, s3):
     slots, size, depth, inner = tiles.shape
     width = s2.shape[1]
     dma = pltpu.SemaphoreType.DMA
     hbm = pl.BlockSpec(memory_space=pltpu.HBM)
     return pl.pallas_call(
-        rows_kernel,
-        out_shape=[jax.ShapeDtypeStruct((size, width), F32), jax.ShapeDtypeStruct((2, width, 128), F32)],
+        functools.partial(rows_kernel, scale),
+        out_shape=jax.ShapeDtypeStruct((size, width), F32),
         in_specs=[hbm] * 7,
-        out_specs=[pl.BlockSpec(memory_space=VMEM)] * 2,
+        out_specs=pl.BlockSpec(memory_space=VMEM),
         scratch_shapes=[
+            VMEM((size, width), F32),
+            VMEM((2, width, 128), F32),
+            VMEM((width, width), F32),
             VMEM(f2.shape, BF),
             VMEM(s2.shape, BF),
             VMEM(f3.shape, BF),
             VMEM(s3.shape, BF),
             VMEM(tiles.shape, BF),
             VMEM((slots, depth * size, inner), BF),
-            VMEM((2 * NX * NY, 2, f2.shape[0] // PARTS, width), BF),
+            VMEM((2 * NX * NY, PARTS // 2, f2.shape[0] // PARTS, width), BF),
             VMEM((2, size * depth // 2, inner), F32),
             VMEM((slots, size, width), F32),
             VMEM((slots, size, width), F32),
@@ -336,23 +353,22 @@
             VMEM((NZ, size, width), BF),
             VMEM((4, 4, size, 128), BF),
             VMEM((4, 4, size, 128), BF),
+            VMEM((size, width), F32),
             VMEM((width, 128), F32),
-            VMEM((width, 128), F32),
-            VMEM((1, width, 128), F32),
             VMEM((NX, NY, 8, 128), F32),
             VMEM((NZ, 8, 128), F32),
             dma((6,)), dma((slots,)),
             dma((31, PARTS)), dma((31, PARTS)),
             dma((NZ,)), dma((NZ,)),
             dma((4, 4, CUTS)), dma((4, 4, CUTS)),
-            dma, dma,
+            dma((CUTS,)), dma((CUTS,)),
             dma((NX, NY)), dma((NX, NY)),
             dma((NZ,)), dma((NZ,)),
             dma((NX, NY)), dma((NX, NY)),
             dma((NX,)), dma((NX,)),
         ],
         compiler_params=pltpu.CompilerParams(collective_id=0, has_side_effects=True, vmem_limit_bytes=63 * MIB),
-        name="new_rows",
+        name="new_factor",
     )(coords, count, tiles, f2, s2, f3, s3)
 
 
@@ -362,39 +378,39 @@
     lane = lax.broadcasted_iota(jnp.int32, (sub, 128), 1)
     parts, groups = size // sub, n // 128
     home, off = base // 128, base % 128
-    panel = [[work[pl.ds(base + c * sub, sub), pl.ds(g * 128, 128)] for c in range(parts)] for g in range(groups)]
-    block = list(panel[home])
+    panel = []
     for c in range(parts):
+        cut = [work[pl.ds(base + c * sub, sub), pl.ds(g * 128, 128)] for g in range(groups)]
         unit = jnp.where(lane == off + c * sub + row, 1.0, 0.0)
-        panel[home][c] = jnp.where((lane >= off) & (lane < off + size), unit, block[c])
-    diag = [None] * parts
-
-    def spread(v, j):
-        return jnp.broadcast_to(v[j:j + 1, :], (sub, 128))
-
+        own = cut[home]
+        cut[home] = jnp.where((lane >= off) & (lane < off + size), unit, own)
+        panel.append(jnp.stack(cut + [own]))
+    diag = []
     for s in range(parts):
         below = range(s, parts)
         first = off + s * sub
-        cols = {c: [jnp.broadcast_to(block[c][:, first + k:first + k + 1], (sub, 128)) for k in range(sub)] for c in below}
-        diag[s] = jnp.ones((sub, 128), F32)
+        cols = {c: jnp.stack([jnp.broadcast_to(panel[c][groups][:, first + k:first + k + 1], (sub, 128)) for k in range(sub)])
+                for c in below}
+        if s == parts - 1:
+            panel = [p[:groups] for p in panel]
+        pivots = jnp.ones((sub, 128), F32)
         for j in range(sub):
-            pivot = spread(cols[s][j], j)
+            pivot = jnp.broadcast_to(cols[s][0, j:j + 1], (sub, 128))
             inv = 1.0 / pivot
-            mult = {c: cols[c][j] * inv for c in below}
+            mult = {c: cols[c][0] * inv for c in below}
             mult[s] = jnp.where(row > j, mult[s], 0.0)
-            diag[s] = jnp.where(row == j, pivot, diag[s])
-            for k in range(j + 1, sub):
-                top = spread(cols[s][k], j)
-                for c in below:
-                    cols[c][k] = cols[c][k] - mult[c] * top
-            for g in panel + ([block] if s < parts - 1 else []):
-                top = spread(g[s], j)
-                for c in below:
-                    g[c] = g[c] - mult[c] * top
+            pivots = jnp.where(row == j, pivot, pivots)
+            if j < sub - 1:
+                top = cols[s][1:, j:j + 1]
+                cols = {c: cols[c][1:] - mult[c][None] * top for c in below}
+            top = panel[s][:, j:j + 1]
+            for c in below:
+                panel[c] = panel[c] - mult[c][None] * top
+        diag.append(pivots)
     for c in range(parts):
-        scale = lax.rsqrt(diag[c])
+        scaled = panel[c] * lax.rsqrt(diag[c])[None]
         for g in range(groups):
-            work[pl.ds(base + c * sub, sub), pl.ds(g * 128, 128)] = panel[g][c] * scale
+            work[pl.ds(base + c * sub, sub), pl.ds(g * 128, 128)] = scaled[g]
 
 
 def inverse_factor(work, size):
@@ -423,37 +439,10 @@
         work[pl.ds(base, size), :] = jnp.where(lane <= row, work[pl.ds(base, size), :], 0.0)
 
 
-def solve_kernel(scale, gram_hbm, rows_hbm, out_ref, work, rows, sem):
-    copies = [pltpu.make_async_copy(gram_hbm.at[h], work.at[:, pl.ds(h * 128, 128)], sem.at[h]) for h in range(2)]
-    copies.append(pltpu.make_async_copy(rows_hbm, rows, sem.at[2]))
-    for cp in copies:
-        cp.start()
-    copies[0].wait()
-    copies[1].wait()
-    inverse_factor(work, 32)
-    copies[2].wait()
-    out = lax.dot_general(rows[...], work[...], (((1,), (1,)), ((), ())), precision=lax.Precision.HIGHEST,
-                          preferred_element_type=F32)
-    out_ref[...] = out * scale
-
-
-def solve(gram, rows, scale):
-    n = gram.shape[1]
-    return pl.pallas_call(
-        functools.partial(solve_kernel, scale),
-        out_shape=jax.ShapeDtypeStruct(rows.shape, F32),
-        in_specs=[pl.BlockSpec(memory_space=pltpu.HBM)] * 2,
-        out_specs=pl.BlockSpec(memory_space=VMEM),
-        scratch_shapes=[VMEM((n, n), F32), VMEM(rows.shape, F32), pltpu.SemaphoreType.DMA((3,))],
-        compiler_params=pltpu.CompilerParams(vmem_limit_bytes=63 * MIB),
-        name="solve",
-    )(gram, rows)
-
-
 def per_device(tiles, tile_coords, tile_counts, factor_two, factor_three, sketch_two, sketch_three):
-    rows, gram = new_rows(tile_coords[0, 0].T, tile_counts, tiles[0, 0], factor_two, factor_three, sketch_two, sketch_three)
-    total_rows = rows.shape[0] * lax.axis_size("rows") * lax.axis_size("cols")
-    return solve(gram, rows, float(total_rows) ** 0.5)
+    total_rows = tiles.shape[3] * lax.axis_size("rows") * lax.axis_size("cols")
+    return new_factor(float(total_rows) ** 0.5, tile_coords[0, 0].T, tile_counts, tiles[0, 0], factor_two, factor_three,
+                      sketch_two, sketch_three)
 
 
 def solution(mesh):

time: 92.9 us -> 90.7 us (0.976)
  Pallas kernels: 91.9 us -> 88.3 us
  local copies, waits for them, and re-layouts: 0 us -> 1.57 us
    pallas_call x2 -> x1, Pallas kernels: 91.9 us -> 88.3 us  [new_factor(): pl.pallas_call(functools.partial(rows_kernel, scale), out_shape=jax.Shape...]
    unnamed x0 -> x1, local copies, waits for them, and re-layouts: none -> 1.57 us
where the time goes in v3:
time: 90.7 us; the launch traced here: 90.5 us
  Pallas kernels  88.3 us (97%)
  local copies, waits for them, and re-layouts  1.57 us (2%)
    pallas_call x1, Pallas kernels, new_factor(): pl.pallas_call(functools.partial(rows_kernel, scale), out_shape=jax.Shape...  88.3 us

profile of v3, /device:TPU:1, one launch (start us, length us, event | category | flops | bytes accessed | tf_op | source)
XLA Modules:
  0.0 90.5 jit_solution(9803697275134973816)
XLA Ops:
  0.7 88.3 %new_factor.1 = f32[128,256]{1,0:T(8,128)} custom-call(s32[2,16]{1,0:T(2,128)} %bitcast.5, s32[1,1,1]{2,1,0:T(1,128)S(6)} %copy.9.count_hbm, bf16[16,128,8,128]{3,2,1,0:T(8,128)(2,1)} %bitcast.4, bf16[256,256]{1,0:T(8,128)(2,1)} %f2_hbm.1, bf16[256,256]{1,0:T(8,128)(2,1)} %s2_hbm.1, bf16[8,256]{1,0:T(8,128)(2,1)} %f3_hbm.1, bf16[256,256]{1,0:T(8,128)(2,1)} %s3_hbm.1), custom_call_target="tpu_custom_call" | custom-call | tf_op jit(solution)/shard_map/new_factor/pallas_call | solution.py:330
  88.9 1.6 %copy.10 = f32[128,256]{1,0:T(8,128)} copy(f32[128,256]{1,0:T(8,128)} %new_factor.1) | data formatting | bytes 262144

commit v4 on v3

--- a/solution.py
+++ b/solution.py
@@ -107,7 +107,7 @@
 
 
 def rows_kernel(scale, coords_hbm, count_hbm, tiles_hbm, f2_hbm, s2_hbm, f3_hbm, s3_hbm, out_ref,
-                rows_ref, gram_ref, work, f2_ref, s2_ref, f3_ref, s3_ref, raw, tiles_ref, grouped, flat, terms, sums_ref, coords, count, table,
+                rows_ref, gram_ref, work, f2_ref, s2_ref, f3_ref, s3_ref, raw, tiles_ref, grouped, flat, sums_ref, coords, count, table,
                 pair_out, pair_in, hop_out, hop_in, rows_in, own, plane_in, zin,
                 l_sem, t_sem, s_gather, r_gather,
                 s_pair, r_pair, s_hop, r_hop, s_g, r_g, s_x, r_x, s_z, r_z, s_y, r_y, s_pa, r_pa):
@@ -191,22 +191,27 @@
     for i in range(todo):
         at = min(2 + i, 8 * PARTS - 1)
         between[at] = (lambda f, i=i: (lambda: (f(), reorder(i))))(between[at])
+    weights = []
+
+    def depth_weights():
+        local[4].wait()
+        local[5].wait()
+        weights.append(jnp.dot(f3_ref[...], s3_ref[...], preferred_element_type=F32).astype(BF).astype(F32))
+
+    between[0] = depth_weights
     between[1] = order_slots
     gathers = gather_rows((x, y, c), grouped, s_gather, r_gather, between)
 
-    local[4].wait()
-    local[5].wait()
-    weight = jnp.dot(f3_ref[...], s3_ref[...], preferred_element_type=F32).astype(BF).astype(F32)
-    for s in range(slots):
+    weight = weights[0]
+    total = None
+    for k in range(slots):
+        s = table[0, k]
         sel = grouped[coords[1, s]].reshape(size, weight.shape[1])
         term = None
-        for k in range(depth):
-            prod = jnp.dot(tiles_ref[s, pl.ds(k * size, size), :], sel, preferred_element_type=F32) * weight[k:k + 1, :]
+        for d in range(depth):
+            prod = jnp.dot(tiles_ref[s, pl.ds(d * size, size), :], sel, preferred_element_type=F32) * weight[d:d + 1, :]
             term = prod if term is None else term + prod
-        terms[s] = term
-    total = None
-    for k in range(slots):
-        total = terms[table[0, k]] if k == 0 else jnp.where(table[1, k] == 1, total, 0.0) + terms[table[0, k]]
+        total = term if k == 0 else jnp.where(table[1, k] == 1, total, 0.0) + term
         sums_ref[k] = total
 
     def partial_rows(b, cols, rows):
@@ -345,7 +350,6 @@
             VMEM((2 * NX * NY, PARTS // 2, f2.shape[0] // PARTS, width), BF),
             VMEM((2, size * depth // 2, inner), F32),
             VMEM((slots, size, width), F32),
-            VMEM((slots, size, width), F32),
             pltpu.SMEM(coords.shape, jnp.int32),
             pltpu.SMEM(count.shape, jnp.int32),
             pltpu.SMEM((4, slots), jnp.int32),

time: 90.7 us -> 90.6 us (level)
  no operation moved by 1% of the time
where the time goes in v4:
time: 90.6 us; the launch traced here: 90.4 us
  Pallas kernels  88.2 us (97%)
  local copies, waits for them, and re-layouts  1.57 us (2%)
    pallas_call x1, Pallas kernels, new_factor(): pl.pallas_call(functools.partial(rows_kernel, scale), out_shape=jax.Shape...  88.2 us

profile of v4, /device:TPU:1, one launch (start us, length us, event | category | flops | bytes accessed | tf_op | source)
XLA Modules:
  0.0 90.4 jit_solution(14408929933088239304)
XLA Ops:
  0.7 88.2 %new_factor.1 = f32[128,256]{1,0:T(8,128)} custom-call(s32[2,16]{1,0:T(2,128)} %bitcast.5, s32[1,1,1]{2,1,0:T(1,128)S(6)} %copy.9.count_hbm, bf16[16,128,8,128]{3,2,1,0:T(8,128)(2,1)} %bitcast.4, bf16[256,256]{1,0:T(8,128)(2,1)} %f2_hbm.1, bf16[256,256]{1,0:T(8,128)(2,1)} %s2_hbm.1, bf16[8,256]{1,0:T(8,128)(2,1)} %f3_hbm.1, bf16[256,256]{1,0:T(8,128)(2,1)} %s3_hbm.1), custom_call_target="tpu_custom_call" | custom-call | tf_op jit(solution)/shard_map/new_factor/pallas_call | solution.py:335
  88.9 1.6 %copy.10 = f32[128,256]{1,0:T(8,128)} copy(f32[128,256]{1,0:T(8,128)} %new_factor.1) | data formatting | bytes 262144
